TPU v7x, 32 devices: a whole 2x2x4 slice. The times are simulated.
32 devices in a mesh: case: 2 (over y), wall: 4 (over z), azim: 4 (over x, core).
Axes of the slice: x: 2, y: 2, z: 4, core: 2. Of those that a mesh axis runs over, the one named last changes fastest.
Arguments:
- state: float32 [12, 2, 32, 512], P(None, 'case', 'wall', 'azim'), parts along dimension 1, may hold values from 0.5 to 1.5
- courant: float32 [2, 32, 512], P('case', 'wall', 'azim'), parts along dimension 0, may hold values from -0.6 to 0.6
- cross_sections: float32 [64], replicated, may hold values from 0.02 to 0.6
- band_fractions: float32 [64], replicated, may hold values from 0.02 to 0.2
- absorb_index: int32 [11, 16], replicated, may hold values from 0 to 63
- band_index: int32 [16], replicated, may hold values from 0 to 63
Outputs:
- new_state: float32 [12, 2, 32, 512], P(None, 'case', 'wall', 'azim'), parts along dimension 1
- wall_flux: float32 [2, 512], P('case', 'azim'), parts along dimension 0
There are 2 independent parts, one for each index of `case`. A program takes and returns all parts, laid end to end along the dimension named above; an argument that names none is the same for every part. Nothing has to cross between parts.
All inputs are finite; a program needn't handle non-finite values.
Results may differ from a plain program's by a relative error of at most 0.0003.
Values sent between devices are 32-bit elements; how exact they have to be, the bound alone decides.
A program may use at most 64 MiB of HBM per device.

v0:
```python
import jax
import jax.numpy as jnp
from jax import lax
from jax.sharding import PartitionSpec as P

KERNEL_WEIGHTS = (0.55, 0.45)
KERNEL_RATES = (1.15, 3.4)
FILTER_STRENGTH = 0.02
COUPLING = 0.1


def with_halo(block, sides, width):
    for axis, dim in sides:
        count = lax.axis_size(axis)
        forward = [(i, i + 1) for i in range(count - 1)]
        forward.append((count - 1, 0))
        backward = [(target, source) for source, target in forward]
        low = lax.ppermute(
            lax.slice_in_dim(block, block.shape[dim] - width, None, axis=dim), axis, forward
        )
        high = lax.ppermute(lax.slice_in_dim(block, 0, width, axis=dim), axis, backward)
        block = jnp.concatenate([low, block, high], axis=dim)
    return block


def band_tables(absorb_index, band_index, cross_sections, band_fractions):
    entries = cross_sections.shape[0]
    table_slots = lax.broadcasted_iota(jnp.int32, (1, 1, entries), 2)
    spectral_absorber_area = jnp.sum(
        jnp.where(absorb_index[:, :, None] == table_slots, cross_sections[None, None, :], 0.0),
        axis=2,
    )
    chosen_values = jnp.where(band_index[:, None] == table_slots[0], band_fractions[None, :], 0.0)
    return (spectral_absorber_area, jnp.sum(chosen_values, axis=1))


def viewing_line_irradiance(
    kinetic_heat_level,
    species_concentrations,
    spectral_absorber_area,
    spectral_fraction_weight,
    mesh_cell_width,
    viewing_line_dimension,
):
    absorption = jnp.einsum(
        "kb,kij->bij",
        spectral_absorber_area,
        species_concentrations,
        precision=lax.Precision.HIGHEST,
    )
    optical_thickness_step = absorption * mesh_cell_width
    optical_depth = (
        lax.cumsum(optical_thickness_step, viewing_line_dimension) - 0.5 * optical_thickness_step
    )
    radiated_energy_rate = (
        spectral_fraction_weight[:, None, None]
        * kinetic_heat_level[None] ** 4
        * optical_thickness_step
    )
    net_flux = 0.0
    wall_flux = 0.0
    for weight, decay_rate in zip(KERNEL_WEIGHTS, KERNEL_RATES):
        growth = jnp.exp(decay_rate * optical_depth)
        falloff = jnp.exp(-decay_rate * optical_depth)
        upward = falloff * lax.cumsum(radiated_energy_rate * growth, viewing_line_dimension)
        tail_sum = lax.cumsum(radiated_energy_rate * falloff, viewing_line_dimension, reverse=True)
        net_flux = net_flux + weight * jnp.sum(upward - growth * tail_sum, axis=0)
        wall_flux = wall_flux + weight * jnp.sum(
            lax.index_in_dim(tail_sum, 0, viewing_line_dimension, keepdims=False), axis=0
        )
    return (net_flux, wall_flux)


def edge_pad(net_flux, viewing_line_dimension):
    count = net_flux.shape[viewing_line_dimension]
    first_row = lax.slice_in_dim(net_flux, 0, 1, axis=viewing_line_dimension)
    last_row = lax.slice_in_dim(net_flux, count - 1, count, axis=viewing_line_dimension)
    return jnp.concatenate([first_row, net_flux, last_row], viewing_line_dimension)


def divergence(padded, viewing_line_dimension, mesh_cell_width):
    count = padded.shape[viewing_line_dimension] - 2
    before = lax.slice_in_dim(padded, 0, count, axis=viewing_line_dimension)
    after = lax.slice_in_dim(padded, 2, count + 2, axis=viewing_line_dimension)
    return (before - after) / (2.0 * mesh_cell_width)


def tendency(shifted, courant, heating):
    gradient = (
        45.0 * (shifted(1) - shifted(-1))
        - 9.0 * (shifted(2) - shifted(-2))
        + (shifted(3) - shifted(-3))
    ) / 60.0
    smoothing = (
        shifted(-3)
        + shifted(3)
        - 6.0 * (shifted(-2) + shifted(2))
        + 15.0 * (shifted(-1) + shifted(1))
        - 20.0 * shifted(0)
    )
    change_sum = FILTER_STRENGTH * smoothing - courant[None] * gradient
    return change_sum.at[0].add(COUPLING * heating)


def radiate(current, spectral_absorber_area, spectral_fraction_weight, mesh_cell_width):
    components, stations, row_count, col_count = current.shape
    line_data = jnp.transpose(current, (0, 2, 1, 3)).reshape(
        components, row_count, stations * col_count
    )
    gathered = lax.all_gather(line_data, "wall", axis=1, tiled=True)
    net_flux, wall_flux = viewing_line_irradiance(
        gathered[0],
        gathered[1:],
        spectral_absorber_area,
        spectral_fraction_weight,
        mesh_cell_width,
        1,
    )
    padded = edge_pad(net_flux, 0)
    row_start = lax.axis_index("wall") * row_count
    heating = divergence(
        lax.dynamic_slice_in_dim(padded, row_start, row_count + 2, 0), 0, mesh_cell_width
    )
    heating = jnp.transpose(heating.reshape(row_count, stations, col_count), (1, 0, 2))
    return (heating, wall_flux.reshape(stations, col_count))


def local(state, courant, cross_sections, band_fractions, absorb_index, band_index):
    spectral_absorber_area, spectral_fraction_weight = band_tables(
        absorb_index, band_index, cross_sections, band_fractions
    )
    mesh_cell_width = 1.0 / (state.shape[2] * lax.axis_size("wall"))
    col_count = state.shape[3]

    def segment_change(current):
        heating, wall_flux = radiate(
            current, spectral_absorber_area, spectral_fraction_weight, mesh_cell_width
        )
        padded = with_halo(current, (("azim", 3),), 3)

        def shifted(offset):
            return lax.slice_in_dim(padded, 3 + offset, 3 + offset + col_count, axis=3)

        return (tendency(shifted, courant, heating), wall_flux)

    first_change, first_flux = segment_change(state)
    middle = state + first_change
    second_change, second_flux = segment_change(middle)
    new_state = 0.5 * (state + middle + second_change)
    return (new_state, 0.5 * (first_flux + second_flux))


def solution(mesh):
    return jax.shard_map(
        local,
        mesh=mesh,
        in_specs=(P(None, "case", "wall", "azim"), P("case", "wall", "azim"), P(), P(), P(), P()),
        out_specs=(P(None, "case", "wall", "azim"), P("case", "azim")),
        check_vma=False,
    )
```

profile of v0, /device:TPU:0, one launch (start us, length us, event | category | flops | bytes accessed | tf_op | source)
XLA Modules:
  0.0 42.3 jit_solution(989441874617617582)
XLA Ops:
  0.6 0.0 copy-start
  0.6 1.0 %fusion.71 = (f32[12,1,8,3]{3,2,1,0:T(8,128)S(1)}, f32[12,1,8,3]{3,2,1,0:T(8,128)S(1)}) fusion(f32[12,1,8,128]{3,2,1,0:T(8,128)} %param.10), kind=kLoop, calls=%fused_computation.127 | loop fusion | bytes 4608 | tf_op jit(solution)/shard_map/slice | solution.py:21
  1.6 2.4 %collective-permute-start.1 = (f32[12,1,8,3]{3,2,1,0:T(8,128)S(1)}, f32[12,1,8,3]{3,2,1,0:T(8,128)S(1)}, u32[]{:S(2)}, u32[]{:S(2)}) collective-permute-start(f32[12,1,8,3]{3,2,1,0:T(8,128)S(1)} %get-tuple-element.34), channel_id=1, source_target_pairs={{1,0},{2,1},{3,2},{0,3},{5,4},{6,5},{7,6},{4,7},{9,8},{10,9},{11,1... | collective-permute-start | bytes 3464 | tf_op jit(solution)/shard_map/ppermute | solution.py:21
  4.0 0.0 collective-permute-start
  4.0 0.0 copy-done
  4.0 0.1 copy.53
  4.1 14.1 %all-gather = f32[12,1,32,128]{3,1,0,2:T(1,128)S(1)} all-gather(f32[12,1,8,128]{3,1,0,2:T(1,128)S(1)} %copy.53), channel_id=2, replica_groups=mesh['case'=2,'wall'=4,'azim'=4] {'wall'}, dimensions={2}, use_global_device_ids=true | all-gather | bytes 245760 | tf_op jit(solution)/shard_map/all_gather | solution.py:110
  18.2 0.0 copy-start.1
  18.2 0.0 copy-start.3
  18.3 0.6 %copy-done.1 = s32[11,16]{1,0:T(8,128)S(1)} copy-done((s32[11,16]{1,0:T(8,128)S(1)}, s32[11,16]{1,0:T(8,128)}, u32[]{:S(2)}) %copy-start.1) | copy-done | bytes 728
  18.9 0.0 copy-done.3
  18.9 0.2 select_reduce_fusion
  19.1 0.4 fusion.5
  19.5 0.0 copy-start.4
  19.6 0.0 copy-start.5
  19.6 0.6 %copy-done.4 = f32[64]{0:T(128)S(1)} copy-done((f32[64]{0:T(128)S(1)}, f32[64]{0:T(128)}, u32[]{:S(2)}) %copy-start.4) | copy-done | bytes 280
  20.2 0.0 copy-done.5
  20.2 0.2 select_reduce_fusion.1
  20.4 0.2 fusion.16
  20.7 0.2 fusion.21
  20.9 0.2 fusion.74
  21.1 0.2 fusion.75
  21.4 0.0 copy-start.2
  21.4 0.7 %copy-done.2 = f32[1,8,128]{2,1,0:T(8,128)S(1)} copy-done((f32[1,8,128]{2,1,0:T(8,128)S(1)}, f32[1,8,128]{2,1,0:T(8,128)}, u32[]{:S(2)}) %copy-start.2) | copy-done | bytes 4120
  22.1 0.0 collective-permute-done.1
  22.2 0.0 collective-permute-done
  22.2 0.2 multiply_subtract_fusion.1
  22.4 0.1 copy.56
  22.5 0.1 fusion.70
  22.5 13.8 %all-gather.1 = f32[12,1,32,128]{3,1,0,2:T(1,128)S(1)} all-gather(f32[12,1,8,128]{3,1,0,2:T(1,128)S(1)} %copy.56), channel_id=3, replica_groups=mesh['case'=2,'wall'=4,'azim'=4] {'wall'}, dimensions={2}, use_global_device_ids=true | all-gather | bytes 245760 | tf_op jit(solution)/shard_map/all_gather | solution.py:110
  36.4 0.4 fusion.4
  36.8 0.2 fusion.6
  37.1 0.2 fusion.11
  37.3 0.2 fusion.76
  37.6 0.2 fusion.77
  37.8 0.1 collective-permute-start.3
  37.9 0.5 %collective-permute-start.2 = (f32[12,1,8,3]{3,2,1,0:T(8,128)S(1)}, f32[12,1,8,3]{3,2,1,0:T(8,128)S(1)}, u32[]{:S(2)}, u32[]{:S(2)}) collective-permute-start(f32[12,1,8,3]{3,2,1,0:T(8,128)S(1)} %get-tuple-element.33), channel_id=1, source_target_pairs={{0,1},{1,2},{2,3},{3,0},{4,5},{5,6},{6,7},{7,4},{8,9},{9,10},{10,1... | collective-permute-start | bytes 3464 | tf_op jit(solution)/shard_map/ppermute | solution.py:18
  38.4 0.5 %multiply_bitcast_fusion.1 = f32[1,128]{1,0:T(1,128)} fusion(f32[128]{0:T(128)S(1)} %get-tuple-element.40, f32[128]{0:T(128)S(1)} %get-tuple-element.41, f32[128]{0:T(128)S(1)} %get-tuple-element.42, f32[128]{0:T(128)S(1)} %get-tuple-element.43), kind=kLoop, calls=%fused_computation.115 | loop fusion | flops 1024 | bytes 2560 | tf_op jit(solution)/shard_map/mul | solution.py:150
  38.9 0.7 %collective-permute-done.3 = f32[12,1,8,3]{3,2,1,0:T(8,128)S(1)} collective-permute-done((f32[12,1,8,3]{3,2,1,0:T(8,128)S(1)}, f32[12,1,8,3]{3,2,1,0:T(8,128)S(1)}, u32[]{:S(2)}, u32[]{:S(2)}) %collective-permute-start.3) | collective-permute-done | bytes 1184 | tf_op jit(solution)/shard_map/ppermute | solution.py:21
  39.7 1.8 %collective-permute-done.2 = f32[12,1,8,3]{3,2,1,0:T(8,128)S(1)} collective-permute-done((f32[12,1,8,3]{3,2,1,0:T(8,128)S(1)}, f32[12,1,8,3]{3,2,1,0:T(8,128)S(1)}, u32[]{:S(2)}, u32[]{:S(2)}) %collective-permute-start.2) | collective-permute-done | bytes 1184 | tf_op jit(solution)/shard_map/ppermute | solution.py:18
  41.5 0.2 multiply_subtract_fusion
  41.7 0.6 %add_multiply_fusion = f32[12,1,8,128]{3,2,1,0:T(8,128)} fusion(f32[12,1,8,128]{3,2,1,0:T(8,128)S(1)} %fusion.55, f32[12,1,8,128]{3,2,1,0:T(8,128)S(1)} %copy-done, f32[12,1,8,128]{3,2,1,0:T(8,128)S(1)} %add.105), kind=kLoop, calls=%fused_computation.75 | loop fusion | flops 36864 | bytes 196608 | tf_op jit(solution)/shard_map/mul | solution.py:149
  (20 shorter events, 0.3 us)
Async XLA Ops:
  0.6 3.4 %copy-start = (f32[12,1,8,128]{3,2,1,0:T(8,128)S(1)}, f32[12,1,8,128]{3,2,1,0:T(8,128)}, u32[]{:S(2)}) copy-start(f32[12,1,8,128]{3,2,1,0:T(8,128)} %param.10) | copy-start | bytes 147460
  1.6 20.5 %collective-permute-start.1 = (f32[12,1,8,3]{3,2,1,0:T(8,128)S(1)}, f32[12,1,8,3]{3,2,1,0:T(8,128)S(1)}, u32[]{:S(2)}, u32[]{:S(2)}) collective-permute-start(f32[12,1,8,3]{3,2,1,0:T(8,128)S(1)} %get-tuple-element.34), channel_id=1, source_target_pairs={{1,0},{2,1},{3,2},{0,3},{5,4},{6,5},{7,6},{4,7},{9,8},{10,9},{11,1... | collective-permute-start | bytes 3464 | tf_op jit(solution)/shard_map/ppermute | solution.py:21
  4.0 18.2 %collective-permute-start = (f32[12,1,8,3]{3,2,1,0:T(8,128)S(1)}, f32[12,1,8,3]{3,2,1,0:T(8,128)S(1)}, u32[]{:S(2)}, u32[]{:S(2)}) collective-permute-start(f32[12,1,8,3]{3,2,1,0:T(8,128)S(1)} %get-tuple-element.35), channel_id=1, source_target_pairs={{0,1},{1,2},{2,3},{3,0},{4,5},{5,6},{6,7},{7,4},{8,9},{9,10},{10,1... | collective-permute-start | bytes 3464 | tf_op jit(solution)/shard_map/ppermute | solution.py:18
  18.2 0.7 %copy-start.1 = (s32[11,16]{1,0:T(8,128)S(1)}, s32[11,16]{1,0:T(8,128)}, u32[]{:S(2)}) copy-start(s32[11,16]{1,0:T(8,128)} %param.14) | copy-start | bytes 2116
  18.2 0.7 %copy-start.3 = (f32[64]{0:T(128)S(1)}, f32[64]{0:T(128)}, u32[]{:S(2)}) copy-start(f32[64]{0:T(128)} %param.12) | copy-start | bytes 772
  19.5 0.7 %copy-start.4 = (f32[64]{0:T(128)S(1)}, f32[64]{0:T(128)}, u32[]{:S(2)}) copy-start(f32[64]{0:T(128)} %param.13) | copy-start | bytes 772
  19.6 0.7 %copy-start.5 = (s32[16]{0:T(128)S(1)}, s32[16]{0:T(128)}, u32[]{:S(2)}) copy-start(s32[16]{0:T(128)} %param.15) | copy-start | bytes 196
  21.4 0.7 %copy-start.2 = (f32[1,8,128]{2,1,0:T(8,128)S(1)}, f32[1,8,128]{2,1,0:T(8,128)}, u32[]{:S(2)}) copy-start(f32[1,8,128]{2,1,0:T(8,128)} %param.11) | copy-start | bytes 12292
  37.8 1.8 %collective-permute-start.3 = (f32[12,1,8,3]{3,2,1,0:T(8,128)S(1)}, f32[12,1,8,3]{3,2,1,0:T(8,128)S(1)}, u32[]{:S(2)}, u32[]{:S(2)}) collective-permute-start(f32[12,1,8,3]{3,2,1,0:T(8,128)S(1)} %get-tuple-element.32), channel_id=1, source_target_pairs={{1,0},{2,1},{3,2},{0,3},{5,4},{6,5},{7,6},{4,7},{9,8},{10,9},{11,1... | collective-permute-start | bytes 3464 | tf_op jit(solution)/shard_map/ppermute | solution.py:21
  37.9 3.6 %collective-permute-start.2 = (f32[12,1,8,3]{3,2,1,0:T(8,128)S(1)}, f32[12,1,8,3]{3,2,1,0:T(8,128)S(1)}, u32[]{:S(2)}, u32[]{:S(2)}) collective-permute-start(f32[12,1,8,3]{3,2,1,0:T(8,128)S(1)} %get-tuple-element.33), channel_id=1, source_target_pairs={{0,1},{1,2},{2,3},{3,0},{4,5},{5,6},{6,7},{7,4},{8,9},{9,10},{10,1... | collective-permute-start | bytes 3464 | tf_op jit(solution)/shard_map/ppermute | solution.py:18
where the time goes:
time: 42.6 us; the launch traced here: 42.3 us
  blocking collectives  27.9 us (65%)
  other arithmetic  4.04 us (9%)
  local copies, waits for them, and re-layouts  3.18 us (7%)
  starting transfers between devices  2.94 us (7%)
  waiting for transfers between devices  2.52 us (6%)
  between operations  0.89 us (2%)
  matrix products  0.84 us (2%)
    all_gather x2, blocking collectives, radiate(): gathered = lax.all_gather(line_data, 'wall', axis=1, tiled=True)  27.9 us
    ppermute x2, starting transfers between devices, with_halo(): lax.ppermute(lax.slice_in_dim(block, 0, width, axis=dim), axis, backward)  2.44 us
    unnamed x14, local copies, waits for them, and re-layouts  2 us
    ppermute x2, waiting for transfers between devices, with_halo(): lax.ppermute(lax.slice_in_dim(block, block.shape[dim] - width, None, axis...  1.79 us
    slice x2, local copies, waits for them, and re-layouts, with_halo(): lax.slice_in_dim(block, 0, width, axis=dim)  1.05 us
    another operation x6, other arithmetic, viewing_line_irradiance(): lax.cumsum(optical_thickness_step, viewing_line_dimension)  1.01 us
    another operation x4, other arithmetic, viewing_line_irradiance(): lax.cumsum(radiated_energy_rate * falloff, viewing_line_dimension, revers...  0.98 us
  transfers between devices with their start and end apart: 4, of which 2 were waited for; matrix products, arithmetic and copies ran while one was open for 6% of the time, Pallas kernels for 0%

commit v1 on v0

v1 whole, which is shorter than its diff:
```python
import functools

import jax
import jax.numpy as jnp
from jax import lax
from jax.experimental import pallas as pl
from jax.experimental.pallas import tpu as pltpu
from jax.sharding import PartitionSpec as P

WEIGHTS = (0.55, 0.45)
RATES = (1.15, 3.4)
FILTER = 0.02
COUPLING = 0.1
REACH = 6
MESH = pl.DeviceIdType.MESH
EXACT = lax.Precision.HIGHEST


def loop(count, body, init):
    if count <= 4:
        for i in range(count):
            init = body(i, init)
        return init
    return lax.fori_loop(0, count, body, init)


def kernel(
    walls, azims, state, courant, sections, fractions, absorb, band,
    new_state, wall_out,
    gs, gc, gl, gr, gh, ms, mh, edge_l, edge_r, em, t1, t2, net, net_h, mat,
    table, idx, cs, bf, bi,
    local_sem, s_state, r_state, s_cour, r_cour, s_left, r_left, s_right, r_right,
):
    comps, rows, lanes = state.shape
    species, bands = absorb.shape
    entries = sections.shape[0]
    total = rows * walls
    me = lax.axis_index("wall")
    az = lax.axis_index("azim")
    right, left = lax.rem(az + 1, azims), lax.rem(az + azims - 1, azims)

    def peer(d):
        return lax.rem(me + d, walls)

    def source(d):
        return lax.rem(me + walls - d, walls)

    barrier = pltpu.get_barrier_semaphore()

    def greet(d, _):
        pl.semaphore_signal(barrier, inc=1, device_id={"wall": peer(d), "azim": left}, device_id_type=MESH)
        pl.semaphore_signal(barrier, inc=1, device_id={"wall": peer(d), "azim": right}, device_id_type=MESH)
        return 0

    def greet_wall(d, _):
        pl.semaphore_signal(barrier, inc=1, device_id={"wall": peer(d + 1)}, device_id_type=MESH)
        return 0

    loop(walls - 1, greet_wall, 0)
    loop(walls, greet, 0)

    loads = [
        pltpu.make_async_copy(src, dst, local_sem.at[i])
        for i, (src, dst) in enumerate(
            [(state, gs.at[me]), (courant, gc.at[me]), (sections, cs), (fractions, bf), (absorb, idx), (band, bi)]
        )
    ]
    for c in loads:
        c.start()
    for c in loads[:2]:
        c.wait()

    lane = lax.broadcasted_iota(jnp.int32, (rows, lanes), 1)

    el = jnp.zeros((rows, lanes), jnp.float32)
    er = jnp.zeros((rows, lanes), jnp.float32)
    for c in range(comps + 1):
        x = gs[me, c] if c < comps else gc[me]
        here = (lane >= REACH * c) & (lane < REACH * (c + 1))
        el = jnp.where(here, pltpu.roll(x, REACH * c, 1) if c else x, el)
        er = jnp.where(here, pltpu.roll(x, (REACH * (c + 1)) % lanes, 1), er)
    edge_l[...] = el
    edge_r[...] = er

    pl.semaphore_wait(barrier, 3 * walls - 1)

    def state_copy(d, slot):
        return pltpu.make_async_remote_copy(
            src_ref=state, dst_ref=gs.at[slot], send_sem=s_state.at[d], recv_sem=r_state.at[d],
            device_id={"wall": peer(d)}, device_id_type=MESH)

    def cour_copy(d, slot):
        return pltpu.make_async_remote_copy(
            src_ref=courant, dst_ref=gc.at[slot], send_sem=s_cour.at[d], recv_sem=r_cour.at[d],
            device_id={"wall": peer(d)}, device_id_type=MESH)

    def left_copy(d, slot):
        return pltpu.make_async_remote_copy(
            src_ref=edge_r, dst_ref=gl.at[slot], send_sem=s_left.at[d], recv_sem=r_left.at[d],
            device_id={"wall": peer(d), "azim": right}, device_id_type=MESH)

    def right_copy(d, slot):
        return pltpu.make_async_remote_copy(
            src_ref=edge_l, dst_ref=gr.at[slot], send_sem=s_right.at[d], recv_sem=r_right.at[d],
            device_id={"wall": peer(d), "azim": left}, device_id_type=MESH)

    def send_state(i, _):
        state_copy(i + 1, me).start()
        return 0

    def send_edges(d, _):
        left_copy(d, me).start()
        right_copy(d, me).start()
        return 0

    def send_cour(i, _):
        cour_copy(i + 1, me).start()
        return 0

    loop(walls - 1, send_state, 0)
    loop(walls, send_edges, 0)
    loop(walls - 1, send_cour, 0)

    for c in loads[2:]:
        c.wait()
    index = idx[...]
    picked = lax.fori_loop(
        0, entries, lambda t, acc: jnp.where(index == t, cs[t], acc), jnp.zeros((species, bands), jnp.float32), unroll=8)
    table[...] = jnp.zeros_like(table)
    table[0:species, 0:bands] = picked
    kpad = table.shape[0]
    rb = rows * bands
    spread = jnp.where(
        lax.broadcasted_iota(jnp.int32, (rb, lanes), 0) % bands == lax.broadcasted_iota(jnp.int32, (rb, lanes), 1), 1.0, 0.0)
    by_row = lax.dot_general(spread, table[...], (((1,), (1,)), ((), ())), precision=EXACT, preferred_element_type=jnp.float32)
    cr = comps * rows
    columns = jnp.where(
        lax.broadcasted_iota(jnp.int32, (kpad, cr), 1) // rows == lax.broadcasted_iota(jnp.int32, (kpad, cr), 0) + 1, 1.0, 0.0)
    full = jnp.dot(by_row, columns, precision=EXACT, preferred_element_type=jnp.float32)
    same_row = lax.broadcasted_iota(jnp.int32, (rb, cr), 0) // bands == lax.broadcasted_iota(jnp.int32, (rb, cr), 1) % rows
    mat[...] = jnp.where(same_row, full, 0.0) * (1.0 / total)
    band_row = lax.broadcasted_iota(jnp.int32, (bands, lanes), 0)
    share = jnp.zeros((bands, lanes), jnp.float32)
    for b in range(bands):
        share = jnp.where(band_row == b, bf[bi[b]], share)
    diff_r = lax.broadcasted_iota(jnp.int32, (rows, (rows + 2) * 8), 1) // 8
    diff_i = lax.broadcasted_iota(jnp.int32, (rows, (rows + 2) * 8), 0)
    diff = jnp.where(diff_r == diff_i, 1.0, 0.0) - jnp.where(diff_r == diff_i + 2, 1.0, 0.0)
    heat_scale = COUPLING * total / 2.0

    def cells(ref, z):
        u = ref[z][0:comps].reshape(cr, lanes)
        step = jnp.dot(mat[...], u, precision=EXACT, preferred_element_type=jnp.float32)
        t = ref[z, 0]
        t = t * t
        t = t * t
        t1[z] = jnp.exp(step * (-0.5 * RATES[0]))
        t2[z] = jnp.exp(step * (-0.5 * RATES[1]))
        for r in range(rows):
            part = slice(r * bands, (r + 1) * bands)
            em[z, part] = step[part] * (share * t[r : r + 1])

    def scan(out):
        zero = jnp.zeros((bands, lanes), jnp.float32)

        def fold(a):
            s = a[0:8]
            for k in range(8, bands, 8):
                s = s + a[k : k + 8]
            return s

        def up(z, carry):
            u1, u2, a1, a2 = carry
            for r in range(rows):
                part = slice(r * bands, (r + 1) * bands)
                e, b1, b2 = em[z, part], t1[z, part], t2[z, part]
                u1 = WEIGHTS[0] * e + (a1 * b1) * u1
                u2 = WEIGHTS[1] * e + (a2 * b2) * u2
                out[1 + z * rows + r] = fold(u1 + u2)
                a1, a2 = b1, b2
            return u1, u2, a1, a2

        def down(i, carry):
            d1, d2, a1, a2 = carry
            z = walls - 1 - i
            for r in reversed(range(rows)):
                part = slice(r * bands, (r + 1) * bands)
                e, b1, b2 = em[z, part], t1[z, part], t2[z, part]
                d1 = WEIGHTS[0] * e + (a1 * b1) * d1
                d2 = WEIGHTS[1] * e + (a2 * b2) * d2
                at = 1 + z * rows + r
                out[at] = out[at] - fold(d1 + d2)
                a1, a2 = b1, b2
            return d1, d2, a1, a2

        loop(walls, up, (zero, zero, zero, zero))
        d1, d2, a1, a2 = loop(walls, down, (zero, zero, zero, zero))
        out[0] = out[1]
        out[total + 1] = out[total]
        return jnp.sum(fold(a1 * d1 + a2 * d2), axis=0, keepdims=True)

    def heat(ref, z):
        part = ref[pl.ds(z * rows, rows + 2)].reshape((rows + 2) * 8, lanes)
        return heat_scale * jnp.dot(diff, part, precision=EXACT, preferred_element_type=jnp.float32)

    def shifts(x, h):
        own, halo = {0: x}, {0: h}
        for o in (1, 2, 3, -1, -2, -3):
            rx, rh = pltpu.roll(x, (-o) % lanes, 1), pltpu.roll(h, (-o) % lanes, 1)
            inside = lane < lanes - o if o > 0 else lane >= -o
            own[o] = jnp.where(inside, rx, rh)
            halo[o] = jnp.where(inside, rh, rx)
        return own, halo

    def tendency(s, cour):
        gradient = (45.0 / 60.0) * (s[1] - s[-1]) - (9.0 / 60.0) * (s[2] - s[-2]) + (1.0 / 60.0) * (s[3] - s[-3])
        smooth = (s[-3] + s[3]) - 6.0 * (s[-2] + s[2]) + 15.0 * (s[-1] + s[1]) - 20.0 * s[0]
        return FILTER * smooth - cour * gradient

    def arrive(d, _):
        if isinstance(d, int) and d == 0:
            cells(gs, me)
            return 0
        state_copy(d, source(d)).wait_recv()
        cells(gs, source(d))
        return 0

    cells(gs, me)
    loop(walls - 1, lambda i, _: arrive(i + 1, _), 0)
    flux = scan(net)

    def halos(d, _):
        left_copy(d, source(d)).wait_recv()
        right_copy(d, source(d)).wait_recv()
        z = source(d)
        pr, pk = gr[z], gl[z]
        for c in range(comps + 1):
            a = pltpu.roll(pr, lanes - REACH * c, 1) if c else pr
            b = pltpu.roll(pk, lanes - REACH * (c + 1), 1)
            gh[z, c] = jnp.where(lane < lanes // 2, a, b)
        cells(gh, z)
        return 0

    loop(walls, halos, 0)
    scan(net_h)

    def wait_cour(i, _):
        cour_copy(i + 1, source(i + 1)).wait_recv()
        return 0

    loop(walls - 1, wait_cour, 0)

    def middle(z, _):
        cour = gc[z]
        for c in range(comps):
            x = gs[z, c]
            own, _h = shifts(x, gh[z, c])
            change = tendency(own, cour)
            if c == 0:
                change = change + heat(net, z)
            ms[z, c] = x + change
        cells(ms, z)
        return 0

    loop(walls, middle, 0)
    flux = flux + scan(net)
    wall_out[...] = 0.5 * flux
    hc = gh[me, comps]
    for c in range(comps):
        h = gh[me, c]
        _o, halo = shifts(gs[me, c], h)
        change = tendency(halo, hc)
        if c == 0:
            change = change + heat(net_h, me)
        mh[c] = h + change

    cour = gc[me]
    for c in range(comps):
        x = ms[me, c]
        own, _h = shifts(x, mh[c])
        change = tendency(own, cour)
        if c == 0:
            change = change + heat(net, me)
        new_state[c] = 0.5 * (gs[me, c] + x + change)

    def finish_wall(i, _):
        state_copy(i + 1, me).wait_send()
        cour_copy(i + 1, me).wait_send()
        return 0

    def finish_edges(d, _):
        left_copy(d, me).wait_send()
        right_copy(d, me).wait_send()
        return 0

    loop(walls - 1, finish_wall, 0)
    loop(walls, finish_edges, 0)


def local(walls, azims, state, courant, cross_sections, band_fractions, absorb_index, band_index):
    comps, stations, rows, lanes = state.shape
    bands = absorb_index.shape[1]
    species = absorb_index.shape[0]
    entries = cross_sections.shape[0]
    total = rows * walls
    f32 = jnp.float32
    vmem = pltpu.VMEM
    dma = pltpu.SemaphoreType.DMA
    any_spec = pl.BlockSpec(memory_space=pl.ANY)
    vmem_spec = pl.BlockSpec(memory_space=pltpu.VMEM)
    new_state, wall = pl.pallas_call(
        functools.partial(kernel, walls, azims),
        out_shape=(
            jax.ShapeDtypeStruct((comps, rows, lanes), f32),
            jax.ShapeDtypeStruct((1, lanes), f32),
        ),
        in_specs=[any_spec] * 6,
        out_specs=(vmem_spec, vmem_spec),
        scratch_shapes=[
            vmem((walls, comps, rows, lanes), f32),
            vmem((walls, rows, lanes), f32),
            vmem((walls, rows, lanes), f32),
            vmem((walls, rows, lanes), f32),
            vmem((walls, comps + 1, rows, lanes), f32),
            vmem((walls, comps, rows, lanes), f32),
            vmem((comps, rows, lanes), f32),
            vmem((rows, lanes), f32),
            vmem((rows, lanes), f32),
            vmem((walls, rows * bands, lanes), f32),
            vmem((walls, rows * bands, lanes), f32),
            vmem((walls, rows * bands, lanes), f32),
            vmem((total + 2, 8, lanes), f32),
            vmem((total + 2, 8, lanes), f32),
            vmem((rows * bands, comps * rows), f32),
            vmem((16, lanes), f32),
            vmem((species, bands), jnp.int32),
            pltpu.SMEM((entries,), f32),
            pltpu.SMEM((entries,), f32),
            pltpu.SMEM((bands,), jnp.int32),
            dma((6,)),
        ] + [dma((walls,))] * 8,
        compiler_params=pltpu.CompilerParams(
            collective_id=0, has_side_effects=True, vmem_limit_bytes=48 * 1024 * 1024),
    )(state.reshape(comps, rows, lanes), courant.reshape(rows, lanes), cross_sections, band_fractions, absorb_index, band_index)
    return new_state.reshape(state.shape), wall


def solution(mesh):
    return jax.shard_map(
        functools.partial(local, mesh.shape["wall"], mesh.shape["azim"]),
        mesh=mesh,
        in_specs=(P(None, "case", "wall", "azim"), P("case", "wall", "azim"), P(), P(), P(), P()),
        out_specs=(P(None, "case", "wall", "azim"), P("case", "azim")),
        check_vma=False,
    )
```

time: 42.6 us -> 19.8 us (0.46)
  blocking collectives: 27.9 us -> 0 us
  Pallas kernels: 0 us -> 14.9 us
  other arithmetic: 4.04 us -> 0 us
  starting transfers between devices: 2.94 us -> 0 us
  waiting for transfers between devices: 2.52 us -> 0 us
  matrix products: 0.84 us -> 0 us
  local copies, waits for them, and re-layouts: 3.18 us -> 3.98 us
    all_gather x2 -> x0, blocking collectives: 27.9 us -> none  [radiate(): gathered = lax.all_gather(line_data, 'wall', axis=1, tiled=True)]
    pallas_call x0 -> x1, Pallas kernels: none -> 14.9 us  [local(): pl.pallas_call(functools.partial(kernel, walls, azims), out_shape=(jax.Sh...]
    ppermute x4 -> x0, starting transfers between devices: 2.94 us -> none  [the longest x2 2.44 us: with_halo(): lax.ppermute(lax.slice_in_dim(block, 0, width, axis=dim), axis, backward)]
    ppermute x4 -> x0, waiting for transfers between devices: 2.52 us -> none  [the longest x2 1.79 us: with_halo(): lax.ppermute(lax.slice_in_dim(block, block.shape[dim] - width, None, axis...]
    another operation x10 -> x0, other arithmetic: 1.99 us -> none  [the longest x6 1.01 us: viewing_line_irradiance(): lax.cumsum(optical_thickness_step, viewing_line_dimension)]
    unnamed x14, local copies, waits for them, and re-layouts: 2 us -> 3.98 us
    mul x5 -> x0, other arithmetic: 1.18 us -> none  [the longest x1 0.63 us: local(): new_state = 0.5 * (state + middle + second_change)]
    slice x6 -> x0, local copies, waits for them, and re-layouts: 1.13 us -> none  [the longest x2 1.05 us: with_halo(): lax.slice_in_dim(block, 0, width, axis=dim)]
  transfers between devices with their start and end apart: 4 -> 0, of which waited for: 2 -> 0; matrix products, arithmetic and copies ran while one was open for 6% -> 0% of each run, Pallas kernels for 0% -> 0%
where the time goes in v1:
time: 19.8 us; the launch traced here: 19.5 us
  Pallas kernels  14.9 us (75%)
  local copies, waits for them, and re-layouts  3.98 us (20%)
  between operations  0.67 us (3%)
    pallas_call x1, Pallas kernels, local(): pl.pallas_call(functools.partial(kernel, walls, azims), out_shape=(jax.Sh...  14.9 us
    unnamed x14, local copies, waits for them, and re-layouts  3.98 us

profile of v1, /device:TPU:0, one launch (start us, length us, event | category | flops | bytes accessed | tf_op | source)
XLA Modules:
  0.0 19.5 jit_solution(6700791309886121621)
XLA Ops:
  0.6 0.0 copy-start.3
  0.6 0.0 copy-start.4
  0.7 0.0 copy-start.5
  0.7 0.6 %copy-done.3 = f32[64]{0:T(128)S(1)} copy-done((f32[64]{0:T(128)S(1)}, f32[64]{0:T(128)}, u32[]{:S(2)}) %copy-start.3) | copy-done | bytes 280
  1.3 0.0 copy-done.4
  1.3 0.0 copy-done.5
  1.3 0.0 copy-start
  1.3 0.8 %copy-done = f32[12,1,8,128]{3,2,1,0:T(8,128)S(1)} copy-done((f32[12,1,8,128]{3,2,1,0:T(8,128)S(1)}, f32[12,1,8,128]{3,2,1,0:T(8,128)}, u32[]{:S(2)}) %copy-start) | copy-done | bytes 49176
  2.1 0.0 copy-start.1
  2.1 0.7 %copy-done.1 = s32[11,16]{1,0:T(8,128)S(1)} copy-done((s32[11,16]{1,0:T(8,128)S(1)}, s32[11,16]{1,0:T(8,128)}, u32[]{:S(2)}) %copy-start.1) | copy-done | bytes 728
  2.8 0.0 copy-start.2
  2.8 0.7 %copy-done.2 = f32[1,8,128]{2,1,0:T(8,128)S(1)} copy-done((f32[1,8,128]{2,1,0:T(8,128)S(1)}, f32[1,8,128]{2,1,0:T(8,128)}, u32[]{:S(2)}) %copy-start.2) | copy-done | bytes 4120
  3.5 14.9 %shard_map.77 = (f32[12,8,128]{2,1,0:T(8,128)S(1)}, f32[1,128]{1,0:T(1,128)S(1)}) custom-call(f32[12,8,128]{2,1,0:T(8,128)S(1)} %bitcast.6, f32[8,128]{1,0:T(8,128)S(1)} %bitcast.7, f32[64]{0:T(128)S(1)} %copy-done.3, f32[64]{0:T(128)S(1)} %copy-done.4, s32[11,16]{1,0:T(8,128)S(1)} %copy-done.1, s32[16]{0:T(128)S(1)} %copy-done.5), custom_call_target="tpu_custom_call" | custom-call | tf_op jit(solution)/shard_map/pallas_call | solution.py:311
  18.4 0.6 %copy.11 = f32[12,1,8,128]{3,2,1,0:T(8,128)} copy(f32[12,1,8,128]{3,2,1,0:T(8,128)S(1)} %bitcast.5) | data formatting | bytes 98304
  19.0 0.5 %copy.12 = f32[1,128]{1,0:T(1,128)} copy(f32[1,128]{1,0:T(1,128)S(1)} %get-tuple-element.11) | data formatting | bytes 1024
Async XLA Ops:
  0.6 0.7 %copy-start.3 = (f32[64]{0:T(128)S(1)}, f32[64]{0:T(128)}, u32[]{:S(2)}) copy-start(f32[64]{0:T(128)} %sections.1) | copy-start | bytes 772
  0.6 0.7 %copy-start.4 = (f32[64]{0:T(128)S(1)}, f32[64]{0:T(128)}, u32[]{:S(2)}) copy-start(f32[64]{0:T(128)} %fractions.1) | copy-start | bytes 772
  0.7 0.7 %copy-start.5 = (s32[16]{0:T(128)S(1)}, s32[16]{0:T(128)}, u32[]{:S(2)}) copy-start(s32[16]{0:T(128)} %band.1) | copy-start | bytes 196
  1.3 0.8 %copy-start = (f32[12,1,8,128]{3,2,1,0:T(8,128)S(1)}, f32[12,1,8,128]{3,2,1,0:T(8,128)}, u32[]{:S(2)}) copy-start(f32[12,1,8,128]{3,2,1,0:T(8,128)} %param.6) | copy-start | bytes 147460
  2.1 0.7 %copy-start.1 = (s32[11,16]{1,0:T(8,128)S(1)}, s32[11,16]{1,0:T(8,128)}, u32[]{:S(2)}) copy-start(s32[11,16]{1,0:T(8,128)} %absorb.1) | copy-start | bytes 2116
  2.8 0.7 %copy-start.2 = (f32[1,8,128]{2,1,0:T(8,128)S(1)}, f32[1,8,128]{2,1,0:T(8,128)}, u32[]{:S(2)}) copy-start(f32[1,8,128]{2,1,0:T(8,128)} %param.7) | copy-start | bytes 12292

commit v2 on v1

--- a/solution.py
+++ b/solution.py
@@ -29,7 +29,7 @@
     new_state, wall_out,
     gs, gc, gl, gr, gh, ms, mh, edge_l, edge_r, em, t1, t2, net, net_h, mat,
     table, idx, cs, bf, bi,
-    local_sem, s_state, r_state, s_cour, r_cour, s_left, r_left, s_right, r_right,
+    local_sem, edge_sem, s_state, r_state, s_cour, r_cour,
 ):
     comps, rows, lanes = state.shape
     species, bands = absorb.shape
@@ -47,79 +47,66 @@
 
     barrier = pltpu.get_barrier_semaphore()
 
-    def greet(d, _):
-        pl.semaphore_signal(barrier, inc=1, device_id={"wall": peer(d), "azim": left}, device_id_type=MESH)
-        pl.semaphore_signal(barrier, inc=1, device_id={"wall": peer(d), "azim": right}, device_id_type=MESH)
-        return 0
-
-    def greet_wall(d, _):
-        pl.semaphore_signal(barrier, inc=1, device_id={"wall": peer(d + 1)}, device_id_type=MESH)
-        return 0
-
-    loop(walls - 1, greet_wall, 0)
-    loop(walls, greet, 0)
+    def greet(i, _):
+        pl.semaphore_signal(barrier, inc=1, device_id={"wall": peer(i + 1)}, device_id_type=MESH)
+        return 0
+
+    loop(walls - 1, greet, 0)
+    for side in (left, right):
+        pl.semaphore_signal(barrier, inc=1, device_id={"azim": side}, device_id_type=MESH)
 
     loads = [
         pltpu.make_async_copy(src, dst, local_sem.at[i])
         for i, (src, dst) in enumerate(
-            [(state, gs.at[me]), (courant, gc.at[me]), (sections, cs), (fractions, bf), (absorb, idx), (band, bi)]
+            [(state, gs.at[me]), (courant, gc.at[me, 0]), (sections, cs), (fractions, bf), (absorb, idx), (band, bi)]
         )
     ]
     for c in loads:
         c.start()
+    lane = lax.broadcasted_iota(jnp.int32, (rows, lanes), 1)
+
+    pl.semaphore_wait(barrier, walls + 1)
+
+    def state_copy(d, slot):
+        return pltpu.make_async_remote_copy(
+            src_ref=state, dst_ref=gs.at[slot], send_sem=s_state.at[d], recv_sem=r_state.at[d],
+            device_id={"wall": peer(d)}, device_id_type=MESH)
+
+    def line_copy(d, slot):
+        return pltpu.make_async_remote_copy(
+            src_ref=gc.at[me], dst_ref=gc.at[slot], send_sem=s_cour.at[d], recv_sem=r_cour.at[d],
+            device_id={"wall": peer(d)}, device_id_type=MESH)
+
+    def send_state(i, _):
+        state_copy(i + 1, me).start()
+        return 0
+
+    def send_line(i, _):
+        line_copy(i + 1, me).start()
+        return 0
+
+    loop(walls - 1, send_state, 0)
+
     for c in loads[:2]:
         c.wait()
-
-    lane = lax.broadcasted_iota(jnp.int32, (rows, lanes), 1)
-
     el = jnp.zeros((rows, lanes), jnp.float32)
     er = jnp.zeros((rows, lanes), jnp.float32)
     for c in range(comps + 1):
-        x = gs[me, c] if c < comps else gc[me]
+        x = gs[me, c] if c < comps else gc[me, 0]
         here = (lane >= REACH * c) & (lane < REACH * (c + 1))
         el = jnp.where(here, pltpu.roll(x, REACH * c, 1) if c else x, el)
         er = jnp.where(here, pltpu.roll(x, (REACH * (c + 1)) % lanes, 1), er)
     edge_l[...] = el
     edge_r[...] = er
 
-    pl.semaphore_wait(barrier, 3 * walls - 1)
-
-    def state_copy(d, slot):
-        return pltpu.make_async_remote_copy(
-            src_ref=state, dst_ref=gs.at[slot], send_sem=s_state.at[d], recv_sem=r_state.at[d],
-            device_id={"wall": peer(d)}, device_id_type=MESH)
-
-    def cour_copy(d, slot):
-        return pltpu.make_async_remote_copy(
-            src_ref=courant, dst_ref=gc.at[slot], send_sem=s_cour.at[d], recv_sem=r_cour.at[d],
-            device_id={"wall": peer(d)}, device_id_type=MESH)
-
-    def left_copy(d, slot):
-        return pltpu.make_async_remote_copy(
-            src_ref=edge_r, dst_ref=gl.at[slot], send_sem=s_left.at[d], recv_sem=r_left.at[d],
-            device_id={"wall": peer(d), "azim": right}, device_id_type=MESH)
-
-    def right_copy(d, slot):
-        return pltpu.make_async_remote_copy(
-            src_ref=edge_l, dst_ref=gr.at[slot], send_sem=s_right.at[d], recv_sem=r_right.at[d],
-            device_id={"wall": peer(d), "azim": left}, device_id_type=MESH)
-
-    def send_state(i, _):
-        state_copy(i + 1, me).start()
-        return 0
-
-    def send_edges(d, _):
-        left_copy(d, me).start()
-        right_copy(d, me).start()
-        return 0
-
-    def send_cour(i, _):
-        cour_copy(i + 1, me).start()
-        return 0
-
-    loop(walls - 1, send_state, 0)
-    loop(walls, send_edges, 0)
-    loop(walls - 1, send_cour, 0)
+    edges = [
+        pltpu.make_async_remote_copy(
+            src_ref=src, dst_ref=dst, send_sem=edge_sem.at[2 * i], recv_sem=edge_sem.at[2 * i + 1],
+            device_id={"azim": to}, device_id_type=MESH)
+        for i, (src, dst, to) in enumerate([(edge_r, gl, right), (edge_l, gr, left)])
+    ]
+    for c in edges:
+        c.start()
 
     for c in loads[2:]:
         c.wait()
@@ -131,7 +118,7 @@
     kpad = table.shape[0]
     rb = rows * bands
     spread = jnp.where(
-        lax.broadcasted_iota(jnp.int32, (rb, lanes), 0) % bands == lax.broadcasted_iota(jnp.int32, (rb, lanes), 1), 1.0, 0.0)
+        lax.broadcasted_iota(jnp.int32, (rb, lanes), 0) & (bands - 1) == lax.broadcasted_iota(jnp.int32, (rb, lanes), 1), 1.0, 0.0)
     by_row = lax.dot_general(spread, table[...], (((1,), (1,)), ((), ())), precision=EXACT, preferred_element_type=jnp.float32)
     cr = comps * rows
     columns = jnp.where(
@@ -217,41 +204,41 @@
         smooth = (s[-3] + s[3]) - 6.0 * (s[-2] + s[2]) + 15.0 * (s[-1] + s[1]) - 20.0 * s[0]
         return FILTER * smooth - cour * gradient
 
-    def arrive(d, _):
-        if isinstance(d, int) and d == 0:
-            cells(gs, me)
-            return 0
-        state_copy(d, source(d)).wait_recv()
-        cells(gs, source(d))
-        return 0
-
-    cells(gs, me)
-    loop(walls - 1, lambda i, _: arrive(i + 1, _), 0)
-    flux = scan(net)
-
-    def halos(d, _):
-        left_copy(d, source(d)).wait_recv()
-        right_copy(d, source(d)).wait_recv()
-        z = source(d)
-        pr, pk = gr[z], gl[z]
+    def unpack(z, pr, pk):
         for c in range(comps + 1):
             a = pltpu.roll(pr, lanes - REACH * c, 1) if c else pr
             b = pltpu.roll(pk, lanes - REACH * (c + 1), 1)
             gh[z, c] = jnp.where(lane < lanes // 2, a, b)
         cells(gh, z)
-        return 0
-
-    loop(walls, halos, 0)
+
+    cells(gs, me)
+    for c in edges:
+        c.wait_recv()
+    gc[me, 1] = jnp.where(lane % REACH < REACH // 2, gr[...], gl[...])
+    loop(walls - 1, send_line, 0)
+
+    def arrive(i, _):
+        z = source(i + 1)
+        state_copy(i + 1, z).wait_recv()
+        cells(gs, z)
+        return 0
+
+    loop(walls - 1, arrive, 0)
+    flux = scan(net)
+    unpack(me, gr[...], gl[...])
+
+    def halos(i, _):
+        z = source(i + 1)
+        line_copy(i + 1, z).wait_recv()
+        packed = gc[z, 1]
+        unpack(z, packed, packed)
+        return 0
+
+    loop(walls - 1, halos, 0)
     scan(net_h)
 
-    def wait_cour(i, _):
-        cour_copy(i + 1, source(i + 1)).wait_recv()
-        return 0
-
-    loop(walls - 1, wait_cour, 0)
-
     def middle(z, _):
-        cour = gc[z]
+        cour = gc[z, 0]
         for c in range(comps):
             x = gs[z, c]
             own, _h = shifts(x, gh[z, c])
@@ -274,7 +261,7 @@
             change = change + heat(net_h, me)
         mh[c] = h + change
 
-    cour = gc[me]
+    cour = gc[me, 0]
     for c in range(comps):
         x = ms[me, c]
         own, _h = shifts(x, mh[c])
@@ -283,18 +270,14 @@
             change = change + heat(net, me)
         new_state[c] = 0.5 * (gs[me, c] + x + change)
 
-    def finish_wall(i, _):
+    def finish(i, _):
         state_copy(i + 1, me).wait_send()
-        cour_copy(i + 1, me).wait_send()
-        return 0
-
-    def finish_edges(d, _):
-        left_copy(d, me).wait_send()
-        right_copy(d, me).wait_send()
-        return 0
-
-    loop(walls - 1, finish_wall, 0)
-    loop(walls, finish_edges, 0)
+        line_copy(i + 1, me).wait_send()
+        return 0
+
+    loop(walls - 1, finish, 0)
+    for c in edges:
+        c.wait_send()
 
 
 def local(walls, azims, state, courant, cross_sections, band_fractions, absorb_index, band_index):
@@ -306,7 +289,7 @@
     f32 = jnp.float32
     vmem = pltpu.VMEM
     dma = pltpu.SemaphoreType.DMA
-    any_spec = pl.BlockSpec(memory_space=pl.ANY)
+    hbm_spec = pl.BlockSpec(memory_space=pltpu.HBM)
     vmem_spec = pl.BlockSpec(memory_space=pltpu.VMEM)
     new_state, wall = pl.pallas_call(
         functools.partial(kernel, walls, azims),
@@ -314,13 +297,13 @@
             jax.ShapeDtypeStruct((comps, rows, lanes), f32),
             jax.ShapeDtypeStruct((1, lanes), f32),
         ),
-        in_specs=[any_spec] * 6,
+        in_specs=[hbm_spec] * 6,
         out_specs=(vmem_spec, vmem_spec),
         scratch_shapes=[
             vmem((walls, comps, rows, lanes), f32),
-            vmem((walls, rows, lanes), f32),
-            vmem((walls, rows, lanes), f32),
-            vmem((walls, rows, lanes), f32),
+            vmem((walls, 2, rows, lanes), f32),
+            vmem((rows, lanes), f32),
+            vmem((rows, lanes), f32),
             vmem((walls, comps + 1, rows, lanes), f32),
             vmem((walls, comps, rows, lanes), f32),
             vmem((comps, rows, lanes), f32),
@@ -338,9 +321,10 @@
             pltpu.SMEM((entries,), f32),
             pltpu.SMEM((bands,), jnp.int32),
             dma((6,)),
-        ] + [dma((walls,))] * 8,
+            dma((4,)),
+        ] + [dma((walls,))] * 4,
         compiler_params=pltpu.CompilerParams(
-            collective_id=0, has_side_effects=True, vmem_limit_bytes=48 * 1024 * 1024),
+            collective_id=0, has_side_effects=True, vmem_limit_bytes=58 * 1024 * 1024),
     )(state.reshape(comps, rows, lanes), courant.reshape(rows, lanes), cross_sections, band_fractions, absorb_index, band_index)
     return new_state.reshape(state.shape), wall
 

time: 19.8 us -> 17 us (0.86)
  local copies, waits for them, and re-layouts: 3.98 us -> 1.94 us
  Pallas kernels: 14.9 us -> 14.2 us
    unnamed x14 -> x4, local copies, waits for them, and re-layouts: 3.98 us -> 1.94 us
    pallas_call x1, Pallas kernels: 14.9 us -> 14.2 us  [local(): pl.pallas_call(functools.partial(kernel, walls, azims), out_shape=(jax.Sh...]
where the time goes in v2:
time: 17 us; the launch traced here: 16.8 us
  Pallas kernels  14.2 us (84%)
  local copies, waits for them, and re-layouts  1.94 us (11%)
  between operations  0.65 us (4%)
    pallas_call x1, Pallas kernels, local(): pl.pallas_call(functools.partial(kernel, walls, azims), out_shape=(jax.Sh...  14.2 us
    unnamed x4, local copies, waits for them, and re-layouts  1.94 us

profile of v2, /device:TPU:0, one launch (start us, length us, event | category | flops | bytes accessed | tf_op | source)
XLA Modules:
  0.0 16.8 jit_solution(15905560868092933965)
XLA Ops:
  0.6 14.2 %shard_map.77 = (f32[12,8,128]{2,1,0:T(8,128)}, f32[1,128]{1,0:T(1,128)}) custom-call(f32[12,8,128]{2,1,0:T(8,128)} %bitcast.6, f32[8,128]{1,0:T(8,128)} %bitcast.7, f32[64]{0:T(128)} %sections.1, f32[64]{0:T(128)} %fractions.1, s32[11,16]{1,0:T(8,128)} %absorb.1, s32[16]{0:T(128)} %band.1), custom_call_target="tpu_custom_call" | custom-call | tf_op jit(solution)/shard_map/pallas_call | solution.py:294
  14.8 0.0 copy-start
  14.9 1.4 %copy.11 = f32[12,1,8,128]{3,2,1,0:T(8,128)} copy(f32[12,1,8,128]{3,2,1,0:T(8,128)} %bitcast.5) | data formatting | bytes 98304
  16.3 0.0 copy-done
  16.3 0.5 %copy.12 = f32[1,128]{1,0:T(1,128)} copy(f32[1,128]{1,0:T(1,128)S(1)} %copy-done) | data formatting | bytes 1024
Async XLA Ops:
  14.8 1.4 %copy-start = (f32[1,128]{1,0:T(1,128)S(1)}, f32[1,128]{1,0:T(1,128)}, u32[]{:S(2)}) copy-start(f32[1,128]{1,0:T(1,128)} %get-tuple-element.11) | copy-start | bytes 1540

commit v3 on v2

--- a/solution.py
+++ b/solution.py
@@ -280,6 +280,14 @@
         c.wait_send()
 
 
+def hand_over(a, b, a_out, b_out, sems):
+    copies = [pltpu.make_async_copy(a, a_out, sems.at[0]), pltpu.make_async_copy(b, b_out, sems.at[1])]
+    for c in copies:
+        c.start()
+    for c in copies:
+        c.wait()
+
+
 def local(walls, azims, state, courant, cross_sections, band_fractions, absorb_index, band_index):
     comps, stations, rows, lanes = state.shape
     bands = absorb_index.shape[1]
@@ -294,8 +302,8 @@
     new_state, wall = pl.pallas_call(
         functools.partial(kernel, walls, azims),
         out_shape=(
-            jax.ShapeDtypeStruct((comps, rows, lanes), f32),
-            jax.ShapeDtypeStruct((1, lanes), f32),
+            pltpu.VMEM((comps, rows, lanes), f32),
+            pltpu.VMEM((1, lanes), f32),
         ),
         in_specs=[hbm_spec] * 6,
         out_specs=(vmem_spec, vmem_spec),
@@ -326,6 +334,17 @@
         compiler_params=pltpu.CompilerParams(
             collective_id=0, has_side_effects=True, vmem_limit_bytes=58 * 1024 * 1024),
     )(state.reshape(comps, rows, lanes), courant.reshape(rows, lanes), cross_sections, band_fractions, absorb_index, band_index)
+    hbm = pl.BlockSpec(memory_space=pltpu.HBM)
+    new_state, wall = pl.pallas_call(
+        hand_over,
+        out_shape=(
+            jax.ShapeDtypeStruct((comps, rows, lanes), f32),
+            jax.ShapeDtypeStruct((1, lanes), f32),
+        ),
+        in_specs=[pl.BlockSpec(memory_space=pl.ANY)] * 2,
+        out_specs=(hbm, hbm),
+        scratch_shapes=[dma((2,))],
+    )(pltpu.with_memory_space_constraint(new_state, pltpu.VMEM), pltpu.with_memory_space_constraint(wall, pltpu.VMEM))
     return new_state.reshape(state.shape), wall
 
 

time: 17 us -> 15 us (0.88)
  local copies, waits for them, and re-layouts: 1.94 us -> 0 us
    unnamed x4 -> x0, local copies, waits for them, and re-layouts: 1.94 us -> none
    pallas_call x1 -> x2, Pallas kernels: 14.2 us -> 14.2 us  [the longest x1 13.6 us: local(): pl.pallas_call(functools.partial(kernel, walls, azims), out_shape=(pltpu....]
where the time goes in v3:
time: 15 us; the launch traced here: 14.9 us
  Pallas kernels  14.2 us (95%)
  between operations  0.64 us (4%)
    pallas_call x1, Pallas kernels, local(): pl.pallas_call(functools.partial(kernel, walls, azims), out_shape=(pltpu....  13.6 us
    pallas_call x1, Pallas kernels, local(): pl.pallas_call(hand_over, out_shape=(jax.ShapeDtypeStruct((comps, rows, l...  0.64 us

profile of v3, /device:TPU:0, one launch (start us, length us, event | category | flops | bytes accessed | tf_op | source)
XLA Modules:
  0.0 14.9 jit_solution(14471878367388950500)
XLA Ops:
  0.6 13.6 %shard_map.77 = (f32[12,8,128]{2,1,0:T(8,128)S(1)}, f32[1,128]{1,0:T(1,128)S(1)}) custom-call(f32[12,8,128]{2,1,0:T(8,128)} %bitcast.5, f32[8,128]{1,0:T(8,128)} %bitcast.6, f32[64]{0:T(128)} %sections.1, f32[64]{0:T(128)} %fractions.1, s32[11,16]{1,0:T(8,128)} %absorb.1, s32[16]{0:T(128)} %band.1), custom_call_target="tpu_custom_call" | custom-call | tf_op jit(solution)/shard_map/pallas_call | solution.py:302
  14.2 0.6 %shard_map.78 = (f32[12,8,128]{2,1,0:T(8,128)}, f32[1,128]{1,0:T(1,128)}) custom-call(f32[12,8,128]{2,1,0:T(8,128)S(1)} %get-tuple-element.6.a, f32[1,128]{1,0:T(1,128)S(1)} %get-tuple-element.7.b), custom_call_target="tpu_custom_call" | custom-call | tf_op jit(solution)/shard_map/pallas_call | solution.py:338
